TPU v7x, 128 devices: a whole 4x4x4 slice. The times are simulated.
128 devices in a mesh: front: 8 (over z, x_lo), row: 8 (over x_hi, y), col: 2 (over core).
Axes of the slice: x: 4 (x_hi: 2, x_lo: 2; x = x_hi * 2 + x_lo), y: 4, z: 4, core: 2. Of those that a mesh axis runs over, the one named last changes fastest.
Arguments:
- front_matrix: float32 [8, 12, 1024, 3072], P('front', None, 'row', 'col')
- front_sizes: int32 [8], P('front'), may hold values from 8192 to 12288, as said below
- contrib: float32 [8, 4, 1024, 3072], P('front', None, 'row', 'col'), may hold values from -6 to 6
- dest_front: int32 [8, 4, 8], P('front', None, 'row'), may hold values from 0 to 7, as said below
- dest_local: int32 [8, 4, 8], P('front', None, 'row'), may hold values from 1 to 11, as said below
Outputs:
- factored: float32 [8, 12, 1024, 3072], P('front', None, 'row', 'col')
Inputs may be any that keep to these rules, and one draw needn't show every extreme that they name: `front_sizes`: multiples of 128; every draw has a front of order 12288 and one of order 8192. For each (g, r), the 4 entries dest_front[g, :, r] name distinct fronts. The block (g, k, r) lands on parent rows from (dest_local * 8 + r) * 128: at or after row 1024 and wholly below the parent's order; several blocks may land on the same rows; in every draw some block lands in the last round of blocks of the largest front.
All inputs are finite; a program needn't handle non-finite values.
Results may differ from a plain program's by a relative error of at most 0.0003.
Values sent between devices are 32-bit elements; how exact they have to be, the bound alone decides.
A program may use at most 128 MiB of HBM per device.

v0:
```python
import jax
import jax.numpy as jnp
from jax import lax
from jax.sharding import PartitionSpec as P

PW = 512
NPANEL = 2
W = 3072


def broadcast(value, axis, source):
    kept = jnp.where(lax.axis_index(axis) == source, value, 0).astype(value.dtype)
    return lax.psum(kept, axis)


def lower_inverse(pivot_block):
    symmetric = jnp.tril(pivot_block) + jnp.tril(pivot_block, -1).T
    factor = jnp.linalg.cholesky(symmetric)
    eye_block = jnp.eye(factor.shape[0], dtype=jnp.float32)
    inverse = jax.scipy.linalg.solve_triangular(factor, eye_block, lower=True)
    return (factor, inverse)


def on_device(front_matrix, front_sizes, contrib, dest_front, dest_local):
    front_count = lax.axis_size("front")
    row_count = lax.axis_size("row")
    row_here = lax.axis_index("row")
    col_here = lax.axis_index("col")
    local_blocks = front_matrix.shape[1]
    block_rows = front_matrix.shape[2]
    half_width = front_matrix.shape[3]
    half_rows = block_rows // 2
    cycle_rows = row_count * block_rows
    local_rows = local_blocks * block_rows
    window_blocks = W // cycle_rows
    block_ids = jnp.arange(local_blocks, dtype=jnp.int32)
    global_row = (
        block_ids[:, None] * cycle_rows
        + row_here * block_rows
        + jnp.arange(block_rows, dtype=jnp.int32)[None, :]
    ).reshape(local_rows)
    global_col = col_here * half_width + jnp.arange(half_width, dtype=jnp.int32)
    matrix = front_matrix[0].reshape(local_rows, half_width)
    matrix = jnp.where((global_row < front_sizes[0])[:, None], matrix, 0.0)
    targets = dest_front[0, :, 0]
    places = dest_local[0, :, 0]
    fronts_all = jnp.arange(front_count, dtype=jnp.int32)
    select = targets[None, :] == fronts_all[:, None]
    outgoing = jnp.einsum(
        "fk,kiw->fiw", select.astype(jnp.float32), contrib[0], precision=lax.Precision.HIGHEST
    )
    slot_place = jnp.where(
        jnp.any(select, axis=1), jnp.sum(jnp.where(select, places[None, :], 0), axis=1), -1
    )
    incoming, in_place = (
        lax.all_to_all(outgoing, "front", split_axis=0, concat_axis=0, tiled=True),
        lax.all_to_all(slot_place, "front", split_axis=0, concat_axis=0, tiled=True),
    )
    placing = (in_place[None, :] == block_ids[:, None]).astype(jnp.float32)
    placed_rows = jnp.einsum("ls,siw->liw", placing, incoming, precision=lax.Precision.HIGHEST)
    matrix = matrix + placed_rows.reshape(local_rows, half_width)
    for panel_index in range(NPANEL):
        col_start = panel_index * PW
        owned_columns = matrix[:, col_start : col_start + PW]
        columns = broadcast(owned_columns, "col", 0)
        first_block = col_start // block_rows
        pivot_block = first_block // row_count
        offset = first_block % row_count * block_rows
        col_blocks = columns.reshape(local_blocks, block_rows, PW)
        row_piece = lax.dynamic_slice_in_dim(
            col_blocks[pivot_block], col_here * half_rows, half_rows, 0
        )
        gathered = lax.all_gather(row_piece, ("row", "col"), axis=0, tiled=True)
        factor, inverse = lower_inverse(gathered[offset : offset + PW])
        solved = jnp.dot(columns, inverse.T, precision=lax.Precision.HIGHEST)
        solved = jnp.where((global_row < col_start)[:, None], 0.0, solved)
        global_first = (pivot_block * row_count + row_here) * block_rows
        in_pivot = (global_first >= col_start) & (global_first < col_start + PW)
        pivot_piece = lax.dynamic_slice_in_dim(
            factor, jnp.clip(global_first - col_start, 0, PW - block_rows), block_rows, 0
        )
        current = solved[pivot_block * block_rows : (pivot_block + 1) * block_rows]
        solved = solved.at[pivot_block * block_rows : (pivot_block + 1) * block_rows].set(
            jnp.where(in_pivot, pivot_piece, current)
        )
        solved_blocks = solved.reshape(local_blocks, block_rows, PW)
        row_piece = lax.dynamic_slice_in_dim(
            solved_blocks[:window_blocks], col_here * half_rows, half_rows, 1
        )
        window_factor = lax.all_gather(row_piece, ("row", "col"), axis=1, tiled=True).reshape(W, PW)
        mine_cols = lax.dynamic_slice_in_dim(window_factor, col_here * half_width, half_width, 0)
        update = jnp.dot(solved, mine_cols.T, precision=lax.Precision.HIGHEST)
        active = (global_row >= col_start + PW)[:, None] & (global_col >= col_start + PW)[None, :]
        matrix = matrix - jnp.where(active, update, 0.0)
        replaced = jnp.where(col_here == 0, solved, matrix[:, col_start : col_start + PW])
        matrix = matrix.at[:, col_start : col_start + PW].set(replaced)
    upper_part = (global_row < NPANEL * PW)[:, None] & (global_col >= NPANEL * PW)[None, :]
    matrix = jnp.where(upper_part, 0.0, matrix)
    return matrix.reshape(1, local_blocks, block_rows, half_width)


def solution(mesh):
    return jax.shard_map(
        on_device,
        mesh=mesh,
        in_specs=(
            P("front", None, "row", "col"),
            P("front"),
            P("front", None, "row", "col"),
            P("front", None, "row"),
            P("front", None, "row"),
        ),
        out_specs=P("front", None, "row", "col"),
        check_vma=False,
    )
```

profile of v0, /device:TPU:1, one launch (start us, length us, event | category | flops | bytes accessed | tf_op | source)
XLA Modules:
  0.0 793.3 jit_solution(2299873840947495213)
XLA Ops:
  8.9 6.8 all-to-all-start
  15.7 6.5 fusion.4
  22.2 6.3 copy.24
  28.6 5.1 all-to-all-start.1
  35.2 69.0 %all-to-all-done.1 = f32[8,128,1536]{2,1,0:T(8,128)} async-done(((f32[8,128,1536]{2,1,0:T(8,128)}), f32[8,128,1536]{2,1,0:T(8,128)}, u32[]{:S(2)}, u32[]{:S(2)}) %all-to-all-start.1) | async-done | bytes 6291488 | tf_op jit(solution)/shard_map/all_to_all | solution.py:56
  104.2 12.9 %fusion = f32[12,128,1536]{2,0,1:T(8,128)} fusion(f32[8,128,1536]{2,1,0:T(8,128)} %all-to-all-done.1, s32[8]{0:T(128)S(1)} %reduce.34), kind=kOutput, calls=%fused_computation.9 | convolution fusion | flops 226492512 | bytes 15728672 | tf_op jit(solution)/shard_map/ls,siw->liw/dot_general | solution.py:60
  117.1 13.8 %copy.26 = f32[12,128,1536]{2,1,0:T(8,128)} copy(f32[12,128,1536]{2,0,1:T(8,128)} %fusion) | data formatting | bytes 18874368 | tf_op jit(solution)/shard_map/ls,siw->liw/dot_general | solution.py:60
  130.9 11.0 %bitcast_add_fusion = f32[1536,1536]{1,0:T(8,128)} fusion(f32[12,128,1536]{2,1,0:T(8,128)} %copy.26, f32[1,12,128,1536]{3,2,1,0:T(8,128)} %param.16, pred[1536]{0:T(1024)(128)(4,1)S(1)} %get-tuple-element.120), kind=kLoop, calls=%fused_computation.4 | loop fusion | flops 4718592 | bytes 28313088 | tf_op jit(solution)/shard_map/add | solution.py:61
  141.9 3.9 slice_select_fusion.1
  145.9 30.6 %all-reduce.4.cloned.1.call-done = f32[1536,512]{1,0:T(8,128)} async-done(((f32[1536,512]{1,0:T(8,128)}), f32[1536,512]{1,0:T(8,128)}) %all-reduce.4.cloned.1.call-update) | async-done | bytes 3145744 | tf_op jit(solution)/shard_map/psum | solution.py:13
  178.5 49.5 %all-gather.5.cloned.1.call-done = f32[1024,512]{1,0:T(8,128)} async-done(((f32[64,512]{1,0:T(8,128)}), f32[1024,512]{1,0:T(8,128)}) %all-gather.5.cloned.1.call-update) | async-done | bytes 2097168 | tf_op jit(solution)/shard_map/all_gather | solution.py:73
  229.7 1.4 bitcast_add_fusion.4
  232.7 11.7 %cholesky.286 = f32[128,128]{1,0:T(8,128)S(1)} custom-call(f32[128,128]{1,0:T(8,128)S(1)} %cholesky.426), custom_call_target="Cholesky" | custom-call | tf_op jit(solution)/shard_map/jit(cholesky)/cholesky | solution.py:18
  244.4 9.8 %custom-call.27 = f32[1,128,128]{1,2,0:T(8,128)S(1)} custom-call(f32[1,128,128]{2,1,0:T(8,128)S(1)} %get-tuple-element.114), custom_call_target="InvertDiagBlocksLowerTriangular" | custom-call | tf_op jit(solution)/shard_map/jit(cholesky)/cholesky | solution.py:18
  256.9 11.7 %cholesky.305 = f32[128,128]{1,0:T(8,128)S(1)} custom-call(f32[128,128]{1,0:T(8,128)S(1)} %cholesky.430), custom_call_target="Cholesky" | custom-call | tf_op jit(solution)/shard_map/jit(cholesky)/cholesky | solution.py:18
  268.6 10.0 %custom-call.28 = f32[1,128,128]{1,2,0:T(8,128)S(1)} custom-call(f32[1,128,128]{2,1,0:T(8,128)S(1)} %get-tuple-element.111), custom_call_target="InvertDiagBlocksLowerTriangular" | custom-call | tf_op jit(solution)/shard_map/jit(cholesky)/cholesky | solution.py:18
  280.2 11.7 %cholesky.326 = f32[128,128]{1,0:T(8,128)S(1)} custom-call(f32[128,128]{1,0:T(8,128)S(1)} %cholesky.435), custom_call_target="Cholesky" | custom-call | tf_op jit(solution)/shard_map/jit(cholesky)/cholesky | solution.py:18
  292.7 9.8 %custom-call.29 = f32[1,128,128]{1,2,0:T(8,128)S(1)} custom-call(f32[1,128,128]{2,1,0:T(8,128)S(1)} %get-tuple-element.108), custom_call_target="InvertDiagBlocksLowerTriangular" | custom-call | tf_op jit(solution)/shard_map/jit(cholesky)/cholesky | solution.py:18
  303.9 12.1 %cholesky.343 = f32[128,128]{1,0:T(8,128)S(1)} custom-call(f32[128,128]{1,0:T(8,128)S(1)} %convolution_subtract_fusion.11), custom_call_target="Cholesky" | custom-call | tf_op jit(solution)/shard_map/jit(cholesky)/cholesky | solution.py:18
  321.3 8.4 %while.8 = (s32[]{:T(128)}, f32[512,512]{1,0:T(8,128)S(1)}, s32[4,2]{0,1:T(2,128)S(1)}, f32[4,128,128]{2,1,0:T(8,128)S(1)}, s32[]{:T(128)}) while((s32[]{:T(128)}, f32[512,512]{1,0:T(8,128)S(1)}, s32[4,2]{0,1:T(2,128)S(1)}, f32[4,128,128]{2,1,0:T(8,128)S(1)}, s32[]{:T(128)}) %tuple.74), condition=%wide.while_cond.4, body=%wide.while_body.4.sunk | while | flops 2 | bytes 131181 | solution.py:20
  322.0 1.4 bitcast_dynamic-update-slice_fusion.4
  324.1 1.4 bitcast_dynamic-update-slice_fusion.4
  326.2 1.4 bitcast_dynamic-update-slice_fusion.4
  328.3 1.4 bitcast_dynamic-update-slice_fusion.4
  329.8 39.3 %custom-call.30 = f32[4,128,128]{1,2,0:T(8,128)S(1)} custom-call(f32[4,128,128]{2,1,0:T(8,128)S(1)} %get-tuple-element.69), custom_call_target="InvertDiagBlocksLowerTriangular" | custom-call | tf_op jit(solution)/shard_map/jit(_solve_triangular)/triangular_solve | solution.py:20
  372.2 7.1 convolution_select_fusion.1
  382.1 62.1 %all-gather.7.cloned.1.call-done = f32[3,1024,512]{2,1,0:T(8,128)} async-done(((f32[3,64,512]{2,1,0:T(8,128)}), f32[3,1024,512]{2,1,0:T(8,128)}) %all-gather.7.cloned.1.call-update) | async-done | bytes 6291472 | tf_op jit(solution)/shard_map/all_gather | solution.py:90
  444.2 19.2 %select_subtract_fusion.1 = f32[1536,1536]{1,0:T(8,128)S(1)} fusion(f32[1536,1536]{1,0:T(8,128)} %bitcast_add_fusion, f32[1536,512]{1,0:T(8,128)S(1)} %fusion.46, pred[1536]{0:T(1024)(128)(4,1)S(1)} %fusion.84, pred[1536]{0:T(1024)(128)(4,1)S(1)} %get-tuple-element.119, f32[3072,512]{1,0:T(8,128)} %bitcast.143, s32[]{:T(128)S(6)} %select_n.117), kind=kOutput, calls=%fused_computation.7 | convolution fusion | flops 14502592512 | bytes 25168900 | tf_op jit(solution)/shard_map/dot_general | solution.py:92
  463.4 1.5 fusion.2
  464.9 3.7 copy-done.2
  468.7 2.1 slice_select_fusion
  470.8 26.8 %all-reduce.6.cloned.1.call-done = f32[1536,512]{1,0:T(8,128)} async-done(((f32[1536,512]{1,0:T(8,128)}), f32[1536,512]{1,0:T(8,128)}) %all-reduce.6.cloned.1.call-update) | async-done | bytes 3145744 | tf_op jit(solution)/shard_map/psum | solution.py:13
  500.0 48.7 %all-gather.9.cloned.1.call-done = f32[1024,512]{1,0:T(8,128)} async-done(((f32[64,512]{1,0:T(8,128)}), f32[1024,512]{1,0:T(8,128)}) %all-gather.9.cloned.1.call-update) | async-done | bytes 2097168 | tf_op jit(solution)/shard_map/all_gather | solution.py:73
  550.4 1.4 bitcast_add_fusion.2
  552.4 11.7 %cholesky.358 = f32[128,128]{1,0:T(8,128)S(1)} custom-call(f32[128,128]{1,0:T(8,128)S(1)} %cholesky.439), custom_call_target="Cholesky" | custom-call | tf_op jit(solution)/shard_map/jit(cholesky)/cholesky | solution.py:18
  564.3 9.8 %custom-call.31 = f32[1,128,128]{1,2,0:T(8,128)S(1)} custom-call(f32[1,128,128]{2,1,0:T(8,128)S(1)} %get-tuple-element.104), custom_call_target="InvertDiagBlocksLowerTriangular" | custom-call | tf_op jit(solution)/shard_map/jit(cholesky)/cholesky | solution.py:18
  574.8 11.7 %cholesky.377 = f32[128,128]{1,0:T(8,128)S(1)} custom-call(f32[128,128]{1,0:T(8,128)S(1)} %cholesky.443), custom_call_target="Cholesky" | custom-call | tf_op jit(solution)/shard_map/jit(cholesky)/cholesky | solution.py:18
  587.8 10.2 %custom-call.32 = f32[1,128,128]{1,2,0:T(8,128)S(1)} custom-call(f32[1,128,128]{2,1,0:T(8,128)S(1)} %get-tuple-element.101), custom_call_target="InvertDiagBlocksLowerTriangular" | custom-call | tf_op jit(solution)/shard_map/jit(cholesky)/cholesky | solution.py:18
  598.7 11.7 %cholesky.398 = f32[128,128]{1,0:T(8,128)S(1)} custom-call(f32[128,128]{1,0:T(8,128)S(1)} %cholesky.448), custom_call_target="Cholesky" | custom-call | tf_op jit(solution)/shard_map/jit(cholesky)/cholesky | solution.py:18
  611.1 9.8 %custom-call.33 = f32[1,128,128]{1,2,0:T(8,128)S(1)} custom-call(f32[1,128,128]{2,1,0:T(8,128)S(1)} %get-tuple-element.98), custom_call_target="InvertDiagBlocksLowerTriangular" | custom-call | tf_op jit(solution)/shard_map/jit(cholesky)/cholesky | solution.py:18
  621.5 11.8 %cholesky.415 = f32[128,128]{1,0:T(8,128)S(1)} custom-call(f32[128,128]{1,0:T(8,128)S(1)} %convolution_subtract_fusion.10), custom_call_target="Cholesky" | custom-call | tf_op jit(solution)/shard_map/jit(cholesky)/cholesky | solution.py:18
  637.9 8.1 %while.9 = (s32[]{:T(128)}, f32[512,512]{1,0:T(8,128)S(1)}, s32[4,2]{0,1:T(2,128)S(1)}, f32[4,128,128]{2,1,0:T(8,128)S(1)}, s32[]{:T(128)}) while((s32[]{:T(128)}, f32[512,512]{1,0:T(8,128)S(1)}, s32[4,2]{0,1:T(2,128)S(1)}, f32[4,128,128]{2,1,0:T(8,128)S(1)}, s32[]{:T(128)}) %tuple.92), condition=%wide.while_cond.4.clone, body=%wide.while_body.4.clone.sunk | while | flops 2 | bytes 131181 | solution.py:20
  646.0 39.3 %custom-call.34 = f32[4,128,128]{1,2,0:T(8,128)S(1)} custom-call(f32[4,128,128]{2,1,0:T(8,128)S(1)} %get-tuple-element.70), custom_call_target="InvertDiagBlocksLowerTriangular" | custom-call | tf_op jit(solution)/shard_map/jit(_solve_triangular)/triangular_solve | solution.py:20
  688.5 7.1 convolution_select_fusion
  698.2 62.2 %all-gather.11.cloned.1.call-done = f32[3,1024,512]{2,1,0:T(8,128)} async-done(((f32[3,64,512]{2,1,0:T(8,128)}), f32[3,1024,512]{2,1,0:T(8,128)}) %all-gather.11.cloned.1.call-update) | async-done | bytes 6291472 | tf_op jit(solution)/shard_map/all_gather | solution.py:90
  760.5 19.3 %select_subtract_fusion = f32[1536,1536]{1,0:T(8,128)S(1)} fusion(f32[1536,1536]{1,0:T(8,128)} %copy-done.2, f32[1536,512]{1,0:T(8,128)S(1)} %fusion.44, pred[1536]{0:T(1024)(128)(4,1)S(1)} %fusion.85, pred[1536]{0:T(1024)(128)(4,1)S(1)} %get-tuple-element.117, f32[3072,512]{1,0:T(8,128)} %bitcast.144, s32[]{:T(128)S(6)} %select_n.117), kind=kOutput, calls=%fused_computation.6 | convolution fusion | flops 14502592512 | bytes 25168900 | tf_op jit(solution)/shard_map/dot_general | solution.py:92
  779.8 1.6 fusion.3
  781.4 4.7 and_select_fusion
  (132 shorter events, 50.7 us)
Async XLA Ops:
  6.5 9.2 %copy-start = (f32[1,4,128,1536]{3,2,1,0:T(8,128)S(1)}, f32[1,4,128,1536]{3,2,1,0:T(8,128)}, u32[]{:S(2)}) copy-start(f32[1,4,128,1536]{3,2,1,0:T(8,128)} %param.18) | copy-start | bytes 9437188
  8.9 19.6 %all-to-all-start = ((s32[8,1,1]{2,1,0:T(1,128)}), s32[8,1,1]{2,1,0:T(1,128)S(1)}, u32[]{:S(2)}, u32[]{:S(2)}) async-start(s32[8,1,1]{2,1,0:T(1,128)} %copy.22), calls=%async_computation | async-start | bytes 8192 | tf_op jit(solution)/shard_map/all_to_all | solution.py:57
  28.6 75.7 %all-to-all-start.1 = ((f32[8,128,1536]{2,1,0:T(8,128)}), f32[8,128,1536]{2,1,0:T(8,128)}, u32[]{:S(2)}, u32[]{:S(2)}) async-start(f32[8,128,1536]{2,1,0:T(8,128)} %copy.24), calls=%async_computation.1 | async-start | bytes 12582912 | tf_op jit(solution)/shard_map/all_to_all | solution.py:56
  33.7 142.8 %all-reduce.4.cloned.1.call-start = ((), (), s32[]{:S(2)}) async-start(), calls=%async_computation.2 | async-start | bytes 6291456 | tf_op jit(solution)/shard_map/psum | solution.py:13
  145.8 82.2 %all-gather.5.cloned.1.call-start = ((), (), s32[]{:S(2)}) async-start(), calls=%async_computation.3 | async-start | bytes 2228224 | tf_op jit(solution)/shard_map/all_gather | solution.py:73
  178.1 266.1 %all-gather.7.cloned.1.call-start = ((), (), s32[]{:S(2)}) async-start(), calls=%async_computation.4 | async-start | bytes 6684672 | tf_op jit(solution)/shard_map/all_gather | solution.py:90
  178.5 192.7 %copy-start.3 = (f32[512,512]{1,0:T(8,128)}, f32[512,512]{1,0:T(8,128)S(1)}, u32[]{:S(2)}) copy-start(f32[512,512]{1,0:T(8,128)S(1)} %fusion.27) | copy-start | bytes 3145732
  231.7 1.0 copy-start.5
  381.2 116.3 %all-reduce.6.cloned.1.call-start = ((), (), s32[]{:S(2)}) async-start(), calls=%async_computation.5 | async-start | bytes 6291456 | tf_op jit(solution)/shard_map/psum | solution.py:13
  464.9 3.7 copy-start.2
  470.8 77.9 %all-gather.9.cloned.1.call-start = ((), (), s32[]{:S(2)}) async-start(), calls=%async_computation.6 | async-start | bytes 2228224 | tf_op jit(solution)/shard_map/all_gather | solution.py:73
  499.2 261.2 %all-gather.11.cloned.1.call-start = ((), (), s32[]{:S(2)}) async-start(), calls=%async_computation.7 | async-start | bytes 6684672 | tf_op jit(solution)/shard_map/all_gather | solution.py:90
  586.5 98.8 %copy-start.4 = (f32[512,512]{1,0:T(8,128)S(1)}, f32[512,512]{1,0:T(8,128)}, u32[]{:S(2)}) copy-start(f32[512,512]{1,0:T(8,128)} %copy-done.3) | copy-start | bytes 3145732
  781.4 4.8 copy-start.1
Sparse Core Ops, SparseCore 0:
  145.9 30.4 all-reduce.3
  179.2 48.7 all-gather.4
  381.4 62.7 all-gather.6
  470.9 26.6 all-reduce.5
  499.9 48.7 all-gather.8
  697.6 62.7 all-gather.10
where the time goes:
time: 802 us; the launch traced here: 793 us
  waiting for transfers between devices  349 us (44%)
  other arithmetic  275 us (34%)
  matrix products  85.6 us (11%)
  local copies, waits for them, and re-layouts  50.2 us (6%)
  between operations  20.2 us (3%)
  starting transfers between devices  13.2 us (2%)
    another operation x29, other arithmetic, lower_inverse(): factor = jnp.linalg.cholesky(symmetric)  159 us
    all_gather x2, waiting for transfers between devices, on_device(): lax.all_gather(row_piece, ('row', 'col'), axis=1, tiled=True).reshape(W, PW)  124 us
    all_gather x2, waiting for transfers between devices, on_device(): gathered = lax.all_gather(row_piece, ('row', 'col'), axis=0, tiled=True)  98.2 us
    another operation x5, other arithmetic, lower_inverse(): inverse = jax.scipy.linalg.solve_triangular(factor, eye_block, lower=True)  81.1 us
    all_to_all x1, waiting for transfers between devices, on_device(): lax.all_to_all(outgoing, 'front', split_axis=0, concat_axis=0, tiled=True)  69 us
    psum x2, waiting for transfers between devices, broadcast(): return lax.psum(kept, axis)  57.3 us
    dot_general x2, matrix products, on_device(): update = jnp.dot(solved, mine_cols.T, precision=lax.Precision.HIGHEST)  38.5 us
    another operation x27, local copies, waits for them, and re-layouts, lower_inverse(): inverse = jax.scipy.linalg.solve_triangular(factor, eye_block, lower=True)  16.4 us
  transfers between devices with their start and end apart: 8, of which 7 were waited for; matrix products, arithmetic and copies ran while one was open for 2% of the time, Pallas kernels for 0%

commit v1 on v0

--- a/solution.py
+++ b/solution.py
@@ -87,7 +87,12 @@
         row_piece = lax.dynamic_slice_in_dim(
             solved_blocks[:window_blocks], col_here * half_rows, half_rows, 1
         )
-        window_factor = lax.all_gather(row_piece, ("row", "col"), axis=1, tiled=True).reshape(W, PW)
+        window_factor = jnp.concatenate(
+            lax.all_to_all(
+                jnp.stack([row_piece] * lax.axis_size(("row", "col"))), ("row", "col"), 0, 0
+            ),
+            axis=1,
+        ).reshape(W, PW)
         mine_cols = lax.dynamic_slice_in_dim(window_factor, col_here * half_width, half_width, 0)
         update = jnp.dot(solved, mine_cols.T, precision=lax.Precision.HIGHEST)
         active = (global_row >= col_start + PW)[:, None] & (global_col >= col_start + PW)[None, :]

time: 802 us -> 889 us (1.11)
  waiting for transfers between devices: 349 us -> 405 us
  local copies, waits for them, and re-layouts: 50.2 us -> 62.6 us
  starting transfers between devices: 13.2 us -> 22.5 us
    all_to_all x0 -> x2, waiting for transfers between devices: none -> 169 us  [on_device(): lax.all_to_all(jnp.stack([row_piece] * lax.axis_size(('row', 'col'))), ('...]
    all_gather x2 -> x0, waiting for transfers between devices: 124 us -> none  [on_device(): lax.all_gather(row_piece, ('row', 'col'), axis=1, tiled=True).reshape(W, PW)]
    psum x2, waiting for transfers between devices: 57.3 us -> 68.8 us  [broadcast(): return lax.psum(kept, axis)]
    all_to_all x0 -> x2, starting transfers between devices: none -> 9.44 us  [on_device(): lax.all_to_all(jnp.stack([row_piece] * lax.axis_size(('row', 'col'))), ('...]
where the time goes in v1:
time: 889 us; the launch traced here: 872 us
  waiting for transfers between devices  405 us (46%)
  other arithmetic  275 us (31%)
  matrix products  86.2 us (10%)
  local copies, waits for them, and re-layouts  62.6 us (7%)
  starting transfers between devices  22.5 us (3%)
  between operations  19.8 us (2%)
    all_to_all x2, waiting for transfers between devices, on_device(): lax.all_to_all(jnp.stack([row_piece] * lax.axis_size(('row', 'col'))), ('...  169 us
    another operation x29, other arithmetic, lower_inverse(): factor = jnp.linalg.cholesky(symmetric)  159 us
    all_gather x2, waiting for transfers between devices, on_device(): gathered = lax.all_gather(row_piece, ('row', 'col'), axis=0, tiled=True)  98.7 us
    another operation x5, other arithmetic, lower_inverse(): inverse = jax.scipy.linalg.solve_triangular(factor, eye_block, lower=True)  81.1 us
    all_to_all x1, waiting for transfers between devices, on_device(): lax.all_to_all(outgoing, 'front', split_axis=0, concat_axis=0, tiled=True)  69 us
    psum x2, waiting for transfers between devices, broadcast(): return lax.psum(kept, axis)  68.8 us
    dot_general x2, matrix products, on_device(): update = jnp.dot(solved, mine_cols.T, precision=lax.Precision.HIGHEST)  39.1 us
  transfers between devices with their start and end apart: 8, of which 7 were waited for; matrix products, arithmetic and copies ran while one was open for 2% of the time, Pallas kernels for 0%

profile of v1, /device:TPU:1, one launch (start us, length us, event | category | flops | bytes accessed | tf_op | source)
XLA Modules:
  0.0 871.5 jit_solution(10067522121072970045)
XLA Ops:
  8.9 6.8 all-to-all-start
  15.7 6.5 fusion.4
  22.2 6.3 copy.35
  28.6 5.1 all-to-all-start.1
  35.2 69.0 %all-to-all-done.1 = f32[8,128,1536]{2,1,0:T(8,128)} async-done(((f32[8,128,1536]{2,1,0:T(8,128)}), f32[8,128,1536]{2,1,0:T(8,128)}, u32[]{:S(2)}, u32[]{:S(2)}) %all-to-all-start.1) | async-done | bytes 6291488 | tf_op jit(solution)/shard_map/all_to_all | solution.py:56
  104.2 12.9 %fusion = f32[12,128,1536]{2,0,1:T(8,128)} fusion(f32[8,128,1536]{2,1,0:T(8,128)} %all-to-all-done.1, s32[8]{0:T(128)S(1)} %reduce.34), kind=kOutput, calls=%fused_computation.9 | convolution fusion | flops 226492512 | bytes 15728672 | tf_op jit(solution)/shard_map/ls,siw->liw/dot_general | solution.py:60
  117.1 13.8 %copy.37 = f32[12,128,1536]{2,1,0:T(8,128)} copy(f32[12,128,1536]{2,0,1:T(8,128)} %fusion) | data formatting | bytes 18874368 | tf_op jit(solution)/shard_map/ls,siw->liw/dot_general | solution.py:60
  130.9 11.0 %bitcast_add_fusion = f32[1536,1536]{1,0:T(8,128)} fusion(f32[12,128,1536]{2,1,0:T(8,128)} %copy.37, f32[1,12,128,1536]{3,2,1,0:T(8,128)} %param.16, pred[1536]{0:T(1024)(128)(4,1)S(1)} %get-tuple-element.120), kind=kLoop, calls=%fused_computation.4 | loop fusion | flops 4718592 | bytes 28313088 | tf_op jit(solution)/shard_map/add | solution.py:61
  141.9 3.9 slice_select_fusion.1
  146.1 30.4 %all-reduce.4.cloned.1.call-done = f32[1536,512]{1,0:T(8,128)} async-done(((f32[1536,512]{1,0:T(8,128)}), f32[1536,512]{1,0:T(8,128)}) %all-reduce.4.cloned.1.call-update) | async-done | bytes 3145744 | tf_op jit(solution)/shard_map/psum | solution.py:13
  178.3 49.7 %all-gather.3.cloned.1.call-done = f32[1024,512]{1,0:T(8,128)} async-done(((f32[64,512]{1,0:T(8,128)}), f32[1024,512]{1,0:T(8,128)}) %all-gather.3.cloned.1.call-update) | async-done | bytes 2097168 | tf_op jit(solution)/shard_map/all_gather | solution.py:73
  232.7 11.7 %cholesky.286 = f32[128,128]{1,0:T(8,128)S(1)} custom-call(f32[128,128]{1,0:T(8,128)S(1)} %cholesky.426), custom_call_target="Cholesky" | custom-call | tf_op jit(solution)/shard_map/jit(cholesky)/cholesky | solution.py:18
  244.4 9.8 %custom-call.27 = f32[1,128,128]{1,2,0:T(8,128)S(1)} custom-call(f32[1,128,128]{2,1,0:T(8,128)S(1)} %get-tuple-element.114), custom_call_target="InvertDiagBlocksLowerTriangular" | custom-call | tf_op jit(solution)/shard_map/jit(cholesky)/cholesky | solution.py:18
  256.9 11.7 %cholesky.305 = f32[128,128]{1,0:T(8,128)S(1)} custom-call(f32[128,128]{1,0:T(8,128)S(1)} %cholesky.430), custom_call_target="Cholesky" | custom-call | tf_op jit(solution)/shard_map/jit(cholesky)/cholesky | solution.py:18
  268.6 10.0 %custom-call.28 = f32[1,128,128]{1,2,0:T(8,128)S(1)} custom-call(f32[1,128,128]{2,1,0:T(8,128)S(1)} %get-tuple-element.111), custom_call_target="InvertDiagBlocksLowerTriangular" | custom-call | tf_op jit(solution)/shard_map/jit(cholesky)/cholesky | solution.py:18
  280.2 11.7 %cholesky.326 = f32[128,128]{1,0:T(8,128)S(1)} custom-call(f32[128,128]{1,0:T(8,128)S(1)} %cholesky.435), custom_call_target="Cholesky" | custom-call | tf_op jit(solution)/shard_map/jit(cholesky)/cholesky | solution.py:18
  292.6 9.8 %custom-call.29 = f32[1,128,128]{1,2,0:T(8,128)S(1)} custom-call(f32[1,128,128]{2,1,0:T(8,128)S(1)} %get-tuple-element.108), custom_call_target="InvertDiagBlocksLowerTriangular" | custom-call | tf_op jit(solution)/shard_map/jit(cholesky)/cholesky | solution.py:18
  303.9 12.1 %cholesky.343 = f32[128,128]{1,0:T(8,128)S(1)} custom-call(f32[128,128]{1,0:T(8,128)S(1)} %convolution_subtract_fusion.11), custom_call_target="Cholesky" | custom-call | tf_op jit(solution)/shard_map/jit(cholesky)/cholesky | solution.py:18
  321.3 8.4 while.8
  329.7 39.3 %custom-call.30 = f32[4,128,128]{1,2,0:T(8,128)S(1)} custom-call(f32[4,128,128]{2,1,0:T(8,128)S(1)} %get-tuple-element.69), custom_call_target="InvertDiagBlocksLowerTriangular" | custom-call | tf_op jit(solution)/shard_map/jit(_solve_triangular)/triangular_solve | solution.py:20
  372.2 7.1 convolution_select_fusion.1
  380.5 3.5 stack.4
  384.0 4.6 all-to-all-start.2
  389.4 84.3 %all-to-all-done.2 = f32[16,3,64,512]{3,2,1,0:T(8,128)} async-done(((f32[16,3,64,512]{3,2,1,0:T(8,128)}), f32[16,3,64,512]{3,2,1,0:T(8,128)}, u32[]{:S(2)}, u32[]{:S(2)}) %all-to-all-start.2) | async-done | bytes 6291488 | tf_op jit(solution)/shard_map/all_to_all | solution.py:91
  473.7 3.5 copy.41
  477.2 19.2 %select_subtract_fusion.1 = f32[1536,1536]{1,0:T(8,128)S(1)} fusion(f32[1536,1536]{1,0:T(8,128)} %bitcast_add_fusion, f32[1536,512]{1,0:T(8,128)S(1)} %fusion.46, pred[1536]{0:T(1024)(128)(4,1)S(1)} %fusion.84, pred[1536]{0:T(1024)(128)(4,1)S(1)} %get-tuple-element.119, f32[3072,512]{1,0:T(8,128)S(1)} %bitcast.145, s32[]{:T(128)S(6)} %select_n.117), kind=kOutput, calls=%fused_computation.7 | convolution fusion | flops 14502592512 | bytes 25169924 | tf_op jit(solution)/shard_map/dot_general | solution.py:97
  496.5 1.5 fusion.2
  498.0 3.7 copy-done.2
  501.7 2.1 slice_select_fusion
  504.1 38.3 %all-reduce.6.cloned.1.call-done = f32[1536,512]{1,0:T(8,128)} async-done(((f32[1536,512]{1,0:T(8,128)}), f32[1536,512]{1,0:T(8,128)}) %all-reduce.6.cloned.1.call-update) | async-done | bytes 3145744 | tf_op jit(solution)/shard_map/psum | solution.py:13
  544.6 49.0 %all-gather.5.cloned.1.call-done = f32[1024,512]{1,0:T(8,128)} async-done(((f32[64,512]{1,0:T(8,128)}), f32[1024,512]{1,0:T(8,128)}) %all-gather.5.cloned.1.call-update) | async-done | bytes 2097168 | tf_op jit(solution)/shard_map/all_gather | solution.py:73
  597.2 11.7 %cholesky.358 = f32[128,128]{1,0:T(8,128)S(1)} custom-call(f32[128,128]{1,0:T(8,128)S(1)} %cholesky.439), custom_call_target="Cholesky" | custom-call | tf_op jit(solution)/shard_map/jit(cholesky)/cholesky | solution.py:18
  609.1 9.8 %custom-call.31 = f32[1,128,128]{1,2,0:T(8,128)S(1)} custom-call(f32[1,128,128]{2,1,0:T(8,128)S(1)} %get-tuple-element.104), custom_call_target="InvertDiagBlocksLowerTriangular" | custom-call | tf_op jit(solution)/shard_map/jit(cholesky)/cholesky | solution.py:18
  619.6 11.7 %cholesky.377 = f32[128,128]{1,0:T(8,128)S(1)} custom-call(f32[128,128]{1,0:T(8,128)S(1)} %cholesky.443), custom_call_target="Cholesky" | custom-call | tf_op jit(solution)/shard_map/jit(cholesky)/cholesky | solution.py:18
  633.1 9.8 %custom-call.32 = f32[1,128,128]{1,2,0:T(8,128)S(1)} custom-call(f32[1,128,128]{2,1,0:T(8,128)S(1)} %get-tuple-element.101), custom_call_target="InvertDiagBlocksLowerTriangular" | custom-call | tf_op jit(solution)/shard_map/jit(cholesky)/cholesky | solution.py:18
  643.6 11.7 %cholesky.398 = f32[128,128]{1,0:T(8,128)S(1)} custom-call(f32[128,128]{1,0:T(8,128)S(1)} %cholesky.448), custom_call_target="Cholesky" | custom-call | tf_op jit(solution)/shard_map/jit(cholesky)/cholesky | solution.py:18
  656.0 9.8 %custom-call.33 = f32[1,128,128]{1,2,0:T(8,128)S(1)} custom-call(f32[1,128,128]{2,1,0:T(8,128)S(1)} %get-tuple-element.98), custom_call_target="InvertDiagBlocksLowerTriangular" | custom-call | tf_op jit(solution)/shard_map/jit(cholesky)/cholesky | solution.py:18
  666.4 11.9 %cholesky.415 = f32[128,128]{1,0:T(8,128)S(1)} custom-call(f32[128,128]{1,0:T(8,128)S(1)} %convolution_subtract_fusion.10), custom_call_target="Cholesky" | custom-call | tf_op jit(solution)/shard_map/jit(cholesky)/cholesky | solution.py:18
  682.7 8.1 while.9
  690.9 39.3 %custom-call.34 = f32[4,128,128]{1,2,0:T(8,128)S(1)} custom-call(f32[4,128,128]{2,1,0:T(8,128)S(1)} %get-tuple-element.70), custom_call_target="InvertDiagBlocksLowerTriangular" | custom-call | tf_op jit(solution)/shard_map/jit(_solve_triangular)/triangular_solve | solution.py:20
  733.3 7.1 convolution_select_fusion
  741.6 3.5 stack.5
  745.0 4.8 all-to-all-start.3
  750.5 84.5 %all-to-all-done.3 = f32[16,3,64,512]{3,2,1,0:T(8,128)} async-done(((f32[16,3,64,512]{3,2,1,0:T(8,128)}), f32[16,3,64,512]{3,2,1,0:T(8,128)}, u32[]{:S(2)}, u32[]{:S(2)}) %all-to-all-start.3) | async-done | bytes 6291488 | tf_op jit(solution)/shard_map/all_to_all | solution.py:91
  835.0 3.5 copy.45
  838.5 19.9 %select_subtract_fusion = f32[1536,1536]{1,0:T(8,128)S(1)} fusion(f32[1536,1536]{1,0:T(8,128)} %copy-done.2, f32[1536,512]{1,0:T(8,128)S(1)} %fusion.44, pred[1536]{0:T(1024)(128)(4,1)S(1)} %fusion.85, pred[1536]{0:T(1024)(128)(4,1)S(1)} %get-tuple-element.117, f32[3072,512]{1,0:T(8,128)S(1)} %bitcast.146, s32[]{:T(128)S(6)} %select_n.117), kind=kOutput, calls=%fused_computation.6 | convolution fusion | flops 14502592512 | bytes 25169924 | tf_op jit(solution)/shard_map/dot_general | solution.py:97
  858.4 1.6 fusion.3
  860.0 4.7 and_select_fusion
  (134 shorter events, 57.8 us)
Async XLA Ops:
  6.5 9.2 %copy-start = (f32[1,4,128,1536]{3,2,1,0:T(8,128)S(1)}, f32[1,4,128,1536]{3,2,1,0:T(8,128)}, u32[]{:S(2)}) copy-start(f32[1,4,128,1536]{3,2,1,0:T(8,128)} %param.18) | copy-start | bytes 9437188
  8.9 19.6 %all-to-all-start = ((s32[8,1,1]{2,1,0:T(1,128)}), s32[8,1,1]{2,1,0:T(1,128)S(1)}, u32[]{:S(2)}, u32[]{:S(2)}) async-start(s32[8,1,1]{2,1,0:T(1,128)} %copy.33), calls=%async_computation | async-start | bytes 8192 | tf_op jit(solution)/shard_map/all_to_all | solution.py:57
  28.6 75.7 %all-to-all-start.1 = ((f32[8,128,1536]{2,1,0:T(8,128)}), f32[8,128,1536]{2,1,0:T(8,128)}, u32[]{:S(2)}, u32[]{:S(2)}) async-start(f32[8,128,1536]{2,1,0:T(8,128)} %copy.35), calls=%async_computation.1 | async-start | bytes 12582912 | tf_op jit(solution)/shard_map/all_to_all | solution.py:56
  33.7 142.8 %all-reduce.4.cloned.1.call-start = ((), (), s32[]{:S(2)}) async-start(), calls=%async_computation.4 | async-start | bytes 6291456 | tf_op jit(solution)/shard_map/psum | solution.py:13
  145.8 82.2 %all-gather.3.cloned.1.call-start = ((), (), s32[]{:S(2)}) async-start(), calls=%async_computation.5 | async-start | bytes 2228224 | tf_op jit(solution)/shard_map/all_gather | solution.py:73
  178.3 192.9 %copy-start.3 = (f32[512,512]{1,0:T(8,128)}, f32[512,512]{1,0:T(8,128)S(1)}, u32[]{:S(2)}) copy-start(f32[512,512]{1,0:T(8,128)S(1)} %fusion.27) | copy-start | bytes 3145732
  231.7 1.0 copy-start.5
  384.0 89.8 %all-to-all-start.2 = ((f32[16,3,64,512]{3,2,1,0:T(8,128)}), f32[16,3,64,512]{3,2,1,0:T(8,128)}, u32[]{:S(2)}, u32[]{:S(2)}) async-start(f32[16,3,64,512]{3,2,1,0:T(8,128)} %stack.4), calls=%async_computation.2 | async-start | bytes 12582912 | tf_op jit(solution)/shard_map/all_to_all | solution.py:91
  388.6 153.8 %all-reduce.6.cloned.1.call-start = ((), (), s32[]{:S(2)}) async-start(), calls=%async_computation.6 | async-start | bytes 6291456 | tf_op jit(solution)/shard_map/psum | solution.py:13
  498.0 3.7 copy-start.2
  503.8 89.7 %all-gather.5.cloned.1.call-start = ((), (), s32[]{:S(2)}) async-start(), calls=%async_computation.7 | async-start | bytes 2228224 | tf_op jit(solution)/shard_map/all_gather | solution.py:73
  631.3 98.8 %copy-start.4 = (f32[512,512]{1,0:T(8,128)S(1)}, f32[512,512]{1,0:T(8,128)}, u32[]{:S(2)}) copy-start(f32[512,512]{1,0:T(8,128)} %copy-done.3) | copy-start | bytes 3145732
  745.0 90.0 %all-to-all-start.3 = ((f32[16,3,64,512]{3,2,1,0:T(8,128)}), f32[16,3,64,512]{3,2,1,0:T(8,128)}, u32[]{:S(2)}, u32[]{:S(2)}) async-start(f32[16,3,64,512]{3,2,1,0:T(8,128)} %stack.5), calls=%async_computation.3 | async-start | bytes 12582912 | tf_op jit(solution)/shard_map/all_to_all | solution.py:91
  860.0 4.8 copy-start.1
Sparse Core Ops, SparseCore 0:
  145.9 30.4 all-reduce.3
  179.2 48.7 all-gather.2
  503.9 38.4 all-reduce.5
  544.7 48.7 all-gather.4
